TPU v7x, 32 devices: a whole 2x2x4 slice. The times are simulated.
32 devices in a mesh: grp: 4 (over y, core), tile: 8 (over z, x).
Axes of the slice: x: 2, y: 2, z: 4, core: 2. Of those that a mesh axis runs over, the one named last changes fastest.
Arguments:
- adjoint_state: float32 [64, 128, 2048], P('tile', 'grp'), may hold values from -6 to 6
- misfit: float32 [64, 128, 2048], P('tile', 'grp'), may hold values from -4 to 4
- east_speed: float32 [64, 128, 2048], P('tile', 'grp'), may hold values from -0.6 to 0.6
- north_speed: float32 [64, 128, 2048], P('tile', 'grp'), may hold values from -0.6 to 0.6
- land_mask: int32 [64, 128, 2048], P('tile', 'grp'), may hold values 0 or 1
- warming_forcing_selector: int32 [128, 2048], P('grp', 'tile'), may hold values 0 or 1
- vertical_filter_matrix: float32 [64, 64], replicated, may hold values from 0 to 0.54
Outputs:
- filtered_thermal_sensitivity: float32 [64, 128, 2048], P('tile', 'grp')
- boundary_warming_sensitivity: float32 [128, 2048], P('grp', 'tile')
All inputs are finite; a program needn't handle non-finite values. No bound on the sum of `land_mask` or of `warming_forcing_selector` on one device may be relied on, other than what follows from the above.
Results may differ from a plain program's by a relative error of at most 0.000088.
Values sent between devices are 32-bit elements; how exact they have to be, the bound alone decides.
A program may use at most 192 MiB of HBM per device.

v0:
```python
import jax
import jax.numpy as jnp
from jax import lax
from jax.sharding import PartitionSpec as P

STEPS = 2


def with_halo(cells, sides, width):
    for axis, dim in sides:
        count = lax.axis_size(axis)
        ends = count - 1
        head = lax.slice_in_dim(cells, 0, width, axis=dim)
        tail = lax.slice_in_dim(cells, cells.shape[dim] - width, cells.shape[dim], axis=dim)
        cells = jnp.concatenate(
            [
                lax.ppermute(tail, axis, [(i, (i + 1) % count) for i in range(ends)]),
                cells,
                lax.ppermute(head, axis, [((i + 1) % count, i) for i in range(ends)]),
            ],
            axis=dim,
        )
    return cells


def advance(padded, misfit, east_speed, north_speed, wet_cells):
    center = padded[1:-1, 1:-1, 1:-1]
    east_cell = padded[1:-1, 1:-1, 2:]
    western_neighbour = padded[1:-1, 1:-1, :-2]
    north_cell = padded[1:-1, 2:, 1:-1]
    south_cell = padded[1:-1, :-2, 1:-1]
    upper_cell = padded[:-2, 1:-1, 1:-1]
    lower_cell = padded[2:, 1:-1, 1:-1]
    vertical = upper_cell + lower_cell - 2.0 * center
    lateral = east_cell + western_neighbour + north_cell + south_cell - 4.0 * center
    change = 0.5 * east_speed * (east_cell - western_neighbour) + 0.5 * north_speed * (
        north_cell - south_cell
    )
    return wet_cells * (center + misfit + change + 0.1 * lateral + 0.15 * vertical)


def smooth_levels(vertical_filter_matrix, pencil):
    return jnp.einsum(
        "cz,zne->cne", vertical_filter_matrix, pencil, precision=lax.Precision.HIGHEST
    )


def body(
    adjoint_state,
    misfit,
    east_speed,
    north_speed,
    land_mask,
    warming_forcing_selector,
    vertical_filter_matrix,
):
    wet_cells = land_mask.astype(jnp.float32)
    current_tracer_values = adjoint_state
    for step_index in range(STEPS):
        bordered = with_halo(current_tracer_values, (("grp", 1), ("tile", 0)), 1)
        padded = jnp.pad(bordered, ((0, 0), (0, 0), (1, 1)))
        current_tracer_values = advance(padded, misfit, east_speed, north_speed, wet_cells)
    pencil = lax.all_to_all(current_tracer_values, "tile", split_axis=2, concat_axis=0, tiled=True)
    smoothed_field = smooth_levels(vertical_filter_matrix, pencil)
    surface_layer = smoothed_field[0]
    filtered_thermal_sensitivity = lax.all_to_all(
        smoothed_field, "tile", split_axis=0, concat_axis=2, tiled=True
    )
    boundary_warming_sensitivity = warming_forcing_selector.astype(jnp.float32) * surface_layer
    return (filtered_thermal_sensitivity, boundary_warming_sensitivity)


def solution(mesh):
    in_specs = (
        P("tile", "grp", None),
        P("tile", "grp", None),
        P("tile", "grp", None),
        P("tile", "grp", None),
        P("tile", "grp", None),
        P("grp", "tile"),
        P(),
    )
    out_specs = (P("tile", "grp", None), P("grp", "tile"))
    return jax.shard_map(body, mesh=mesh, in_specs=in_specs, out_specs=out_specs, check_vma=False)
```

profile of v0, /device:TPU:0, one launch (start us, length us, event | category | flops | bytes accessed | tf_op | source)
XLA Modules:
  0.0 217.6 jit_solution(6359021577452492257)
XLA Ops:
  2.1 2.4 %collective-permute-start = (f32[8,1,2048]{2,0,1:T(8,128)S(1)}, f32[8,1,2048]{2,0,1:T(8,128)S(1)}, u32[]{:S(2)}, u32[]{:S(2)}) collective-permute-start(f32[8,1,2048]{2,0,1:T(8,128)S(1)} %copy.101), channel_id=1, source_target_pairs={{0,8},{8,16},{16,24},{1,9},{9,17},{17,25},{2,10},{10,18},{18,26},{... | collective-permute-start | bytes 196616 | tf_op jit(solution)/shard_map/ppermute | solution.py:17
  5.9 3.9 %collective-permute-done.1 = f32[8,1,2048]{2,0,1:T(8,128)S(1)} collective-permute-done((f32[8,1,2048]{2,0,1:T(8,128)S(1)}, f32[8,1,2048]{2,0,1:T(8,128)S(1)}, u32[]{:S(2)}, u32[]{:S(2)}) %collective-permute-start.1) | collective-permute-done | bytes 65568 | tf_op jit(solution)/shard_map/ppermute | solution.py:19
  11.0 3.4 %collective-permute-start.2 = (f32[1,34,2048]{2,1,0:T(8,128)S(1)}, f32[1,34,2048]{2,1,0:T(8,128)S(1)}, u32[]{:S(2)}, u32[]{:S(2)}) collective-permute-start(f32[1,34,2048]{2,1,0:T(8,128)S(1)} %get-tuple-element.4), channel_id=1, source_target_pairs={{0,1},{1,2},{2,3},{3,4},{4,5},{5,6},{6,7},{8,9},{9,10},{10,11},{11... | collective-permute-start | bytes 835592 | tf_op jit(solution)/shard_map/ppermute | solution.py:17
  16.0 4.3 %collective-permute-done.2 = f32[1,34,2048]{2,1,0:T(8,128)S(1)} collective-permute-done((f32[1,34,2048]{2,1,0:T(8,128)S(1)}, f32[1,34,2048]{2,1,0:T(8,128)S(1)}, u32[]{:S(2)}, u32[]{:S(2)}) %collective-permute-start.2) | collective-permute-done | bytes 278560 | tf_op jit(solution)/shard_map/ppermute | solution.py:17
  20.3 5.0 %collective-permute-done.3 = f32[1,34,2048]{2,1,0:T(8,128)S(1)} collective-permute-done((f32[1,34,2048]{2,1,0:T(8,128)S(1)}, f32[1,34,2048]{2,1,0:T(8,128)S(1)}, u32[]{:S(2)}, u32[]{:S(2)}) %collective-permute-start.3) | collective-permute-done | bytes 278560 | tf_op jit(solution)/shard_map/ppermute | solution.py:19
  25.3 3.1 %select_maximum_fusion.4 = f32[10,34,2050]{2,1,0:T(8,128)S(1)} fusion(f32[1,34,2048]{2,1,0:T(8,128)S(1)} %collective-permute-done.3, f32[1,34,2048]{2,1,0:T(8,128)S(1)} %collective-permute-done.2, f32[8,1,2048]{2,1,0:T(1,128)S(1)} %copy.87, f32[8,32,2048]{2,1,0:T(8,128)S(1)} %copy-done.1, f32[8,1,2048]{2,1,0:T(1,128)S(1)} %copy.86), kind=kLoop, calls=%fused_computation.6 | loop fusion | flops 8364000 | bytes 5573280 | tf_op jit(solution)/shard_map/concatenate | solution.py:15
  28.5 4.3 %fusion.10 = f32[8,32,2048]{2,1,0:T(8,128)S(1)} fusion(f32[1,34,2048]{2,1,0:T(8,128)S(1)} %collective-permute-done.3, f32[8,1,2048]{2,1,0:T(1,128)S(1)} %copy.87, f32[8,32,2048]{2,1,0:T(8,128)S(1)} %copy-done.1, f32[8,1,2048]{2,1,0:T(1,128)S(1)} %copy.86, f32[1,34,2048]{2,1,0:T(8,128)S(1)} %collective-permute-done.2, ...), kind=kLoop, calls=%fused_computation.29 | loop fusion | flops 16252928 | bytes 17465344 | tf_op jit(solution)/shard_map/mul | solution.py:39
  32.9 6.2 %collective-permute-start.4 = (f32[8,1,2048]{2,0,1:T(8,128)S(1)}, f32[8,1,2048]{2,0,1:T(8,128)S(1)}, u32[]{:S(2)}, u32[]{:S(2)}) collective-permute-start(f32[8,1,2048]{2,0,1:T(8,128)S(1)} %copy.90), channel_id=1, source_target_pairs={{0,8},{8,16},{16,24},{1,9},{9,17},{17,25},{2,10},{10,18},{18,26},{... | collective-permute-start | bytes 196616 | tf_op jit(solution)/shard_map/ppermute | solution.py:17
  42.5 4.1 %collective-permute-start.6 = (f32[1,34,2048]{2,1,0:T(8,128)S(1)}, f32[1,34,2048]{2,1,0:T(8,128)S(1)}, u32[]{:S(2)}, u32[]{:S(2)}) collective-permute-start(f32[1,34,2048]{2,1,0:T(8,128)S(1)} %get-tuple-element.2), channel_id=1, source_target_pairs={{0,1},{1,2},{2,3},{3,4},{4,5},{5,6},{6,7},{8,9},{9,10},{10,11},{11... | collective-permute-start | bytes 835592 | tf_op jit(solution)/shard_map/ppermute | solution.py:17
  48.0 5.1 %collective-permute-done.6 = f32[1,34,2048]{2,1,0:T(8,128)S(1)} collective-permute-done((f32[1,34,2048]{2,1,0:T(8,128)S(1)}, f32[1,34,2048]{2,1,0:T(8,128)S(1)}, u32[]{:S(2)}, u32[]{:S(2)}) %collective-permute-start.6) | collective-permute-done | bytes 278560 | tf_op jit(solution)/shard_map/ppermute | solution.py:17
  53.1 5.2 %collective-permute-done.7 = f32[1,34,2048]{2,1,0:T(8,128)S(1)} collective-permute-done((f32[1,34,2048]{2,1,0:T(8,128)S(1)}, f32[1,34,2048]{2,1,0:T(8,128)S(1)}, u32[]{:S(2)}, u32[]{:S(2)}) %collective-permute-start.7) | collective-permute-done | bytes 278560 | tf_op jit(solution)/shard_map/ppermute | solution.py:19
  58.3 3.1 %select_maximum_fusion = f32[10,34,2050]{2,1,0:T(8,128)S(1)} fusion(f32[1,34,2048]{2,1,0:T(8,128)S(1)} %collective-permute-done.7, f32[1,34,2048]{2,1,0:T(8,128)S(1)} %collective-permute-done.6, f32[8,1,2048]{2,1,0:T(1,128)S(1)} %copy.93, f32[8,32,2048]{2,1,0:T(8,128)S(1)} %fusion.10, f32[8,1,2048]{2,1,0:T(1,128)S(1)} %copy.92), kind=kLoop, calls=%fused_computation.2 | loop fusion | flops 8364000 | bytes 5573280 | tf_op jit(solution)/shard_map/concatenate | solution.py:15
  61.4 3.0 %fusion.5 = f32[8,32,2048]{2,1,0:T(8,128)S(1)} fusion(f32[1,34,2048]{2,1,0:T(8,128)S(1)} %collective-permute-done.7, f32[8,1,2048]{2,1,0:T(1,128)S(1)} %copy.93, f32[8,32,2048]{2,1,0:T(8,128)S(1)} %fusion.10, f32[8,1,2048]{2,1,0:T(1,128)S(1)} %copy.92, f32[1,34,2048]{2,1,0:T(8,128)S(1)} %collective-permute-done.6, ...), kind=kLoop, calls=%fused_computation.16 | loop fusion | flops 16252928 | bytes 17465344 | tf_op jit(solution)/shard_map/mul | solution.py:39
  64.5 4.7 %copy.96 = f32[8,32,2048]{1,0,2:T(8,128)} copy(f32[8,32,2048]{2,1,0:T(8,128)S(1)} %fusion.5) | data formatting | bytes 4194304 | tf_op jit(solution)/shard_map/mul | solution.py:39
  69.2 7.4 %reshape.5 = f32[8,1,65536]{2,1,0:T(1,128)S(1)} reshape(f32[2048,8,32]{2,1,0:T(8,128)} %bitcast.22) | data formatting | bytes 4194304
  76.6 59.5 %all_to_all.36 = f32[8,1,65536]{2,1,0:T(1,128)} all-to-all(f32[8,1,65536]{2,1,0:T(1,128)S(1)} %reshape.5), channel_id=1, replica_groups=mesh['grp'=4,'tile'=8] {'tile'}, dimensions={0} | all-to-all | bytes 4194304 | tf_op jit(solution)/shard_map/all_to_all | solution.py:63
  136.7 7.2 %reduce = f32[8,65536]{1,0:T(8,128)S(1)} reduce(f32[8,1,65536]{2,1,0:T(1,128)} %all_to_all.36, f32[]{:T(128)} %broadcast.70), dimensions={1}, to_apply=%all_to_all.26.reduce_sub_computation | reduce | bytes 4194308 | tf_op jit(solution)/shard_map/all_to_all | solution.py:63
  143.9 6.0 %reshape.6 = f32[2048,8,32]{2,1,0:T(8,128)} reshape(f32[8,65536]{1,0:T(8,128)S(1)} %reduce) | data formatting | bytes 4194304
  149.9 6.6 %copy.97 = f32[8,32,8,256]{3,0,2,1:T(8,128)} copy(f32[8,32,8,256]{1,0,3,2:T(8,128)} %bitcast.23) | data formatting | bytes 4194304 | tf_op jit(solution)/shard_map/all_to_all | solution.py:63
  156.5 3.6 %fusion.13 = f32[64,32,256]{2,0,1:T(8,128)S(1)} fusion(f32[8,32,8,256]{3,0,2,1:T(8,128)} %copy.97, f32[64,64]{1,0:T(8,128)S(1)} %copy-done), kind=kOutput, calls=%fused_computation.39 | convolution fusion | flops 402653184 | bytes 4210688 | tf_op jit(solution)/shard_map/cz,zne->cne/dot_general | solution.py:43
  160.1 2.5 %copy.98 = f32[64,32,256]{2,1,0:T(8,128)} copy(f32[64,32,256]{2,0,1:T(8,128)S(1)} %fusion.13) | data formatting | bytes 4194304 | tf_op jit(solution)/shard_map/cz,zne->cne/dot_general | solution.py:43
  162.6 4.5 %all-to-all-start.1 = ((f32[64,32,256]{2,1,0:T(8,128)}), f32[64,32,256]{2,1,0:T(8,128)}, u32[]{:S(2)}, u32[]{:S(2)}) async-start(f32[64,32,256]{2,1,0:T(8,128)} %copy.98), calls=%async_computation.1 | async-start | bytes 4194304 | tf_op jit(solution)/shard_map/all_to_all | solution.py:66
  167.8 46.7 %all-to-all-done.1 = f32[64,32,256]{2,1,0:T(8,128)} async-done(((f32[64,32,256]{2,1,0:T(8,128)}), f32[64,32,256]{2,1,0:T(8,128)}, u32[]{:S(2)}, u32[]{:S(2)}) %all-to-all-start.1) | async-done | bytes 2097184 | tf_op jit(solution)/shard_map/all_to_all | solution.py:66
  214.4 3.2 %copy.103 = f32[8,8,4,8,256]{4,3,0,2,1:T(8,128)} copy(f32[8,8,4,8,256]{4,3,2,1,0:T(8,128)} %bitcast.10) | data formatting | bytes 4194304 | tf_op jit(solution)/shard_map/all_to_all | solution.py:66
  (36 shorter events, 11.6 us)
Async XLA Ops:
  0.6 155.8 %copy-start = (f32[64,64]{1,0:T(8,128)S(1)}, f32[64,64]{1,0:T(8,128)}, u32[]{:S(2)}) copy-start(f32[64,64]{1,0:T(8,128)} %param.13) | copy-start | bytes 49156
  0.6 24.7 %copy-start.1 = (f32[8,32,2048]{2,1,0:T(8,128)S(1)}, f32[8,32,2048]{2,1,0:T(8,128)}, u32[]{:S(2)}) copy-start(f32[8,32,2048]{2,1,0:T(8,128)} %param.7) | copy-start | bytes 6291460
  2.1 3.7 %collective-permute-start = (f32[8,1,2048]{2,0,1:T(8,128)S(1)}, f32[8,1,2048]{2,0,1:T(8,128)S(1)}, u32[]{:S(2)}, u32[]{:S(2)}) collective-permute-start(f32[8,1,2048]{2,0,1:T(8,128)S(1)} %copy.101), channel_id=1, source_target_pairs={{0,8},{8,16},{16,24},{1,9},{9,17},{17,25},{2,10},{10,18},{18,26},{... | collective-permute-start | bytes 196616 | tf_op jit(solution)/shard_map/ppermute | solution.py:17
  4.5 5.3 %collective-permute-start.1 = (f32[8,1,2048]{2,0,1:T(8,128)S(1)}, f32[8,1,2048]{2,0,1:T(8,128)S(1)}, u32[]{:S(2)}, u32[]{:S(2)}) collective-permute-start(f32[8,1,2048]{2,0,1:T(8,128)S(1)} %copy.102), channel_id=1, source_target_pairs={{8,0},{16,8},{24,16},{9,1},{17,9},{25,17},{10,2},{18,10},{26,18},{... | collective-permute-start | bytes 196616 | tf_op jit(solution)/shard_map/ppermute | solution.py:19
  11.0 9.3 %collective-permute-start.2 = (f32[1,34,2048]{2,1,0:T(8,128)S(1)}, f32[1,34,2048]{2,1,0:T(8,128)S(1)}, u32[]{:S(2)}, u32[]{:S(2)}) collective-permute-start(f32[1,34,2048]{2,1,0:T(8,128)S(1)} %get-tuple-element.4), channel_id=1, source_target_pairs={{0,1},{1,2},{2,3},{3,4},{4,5},{5,6},{6,7},{8,9},{9,10},{10,11},{11... | collective-permute-start | bytes 835592 | tf_op jit(solution)/shard_map/ppermute | solution.py:17
  14.4 14.0 %copy-start.2 = (f32[8,32,2048]{2,1,0:T(8,128)S(1)}, f32[8,32,2048]{2,1,0:T(8,128)}, u32[]{:S(2)}) copy-start(f32[8,32,2048]{2,1,0:T(8,128)} %param.8) | copy-start | bytes 6291460
  14.4 14.0 %copy-start.3 = (s32[8,32,2048]{2,1,0:T(8,128)S(1)}, s32[8,32,2048]{2,1,0:T(8,128)}, u32[]{:S(2)}) copy-start(s32[8,32,2048]{2,1,0:T(8,128)} %param.11) | copy-start | bytes 6291460
  14.5 14.0 %copy-start.4 = (f32[8,32,2048]{2,1,0:T(8,128)S(1)}, f32[8,32,2048]{2,1,0:T(8,128)}, u32[]{:S(2)}) copy-start(f32[8,32,2048]{2,1,0:T(8,128)} %param.10) | copy-start | bytes 6291460
  14.5 10.9 %collective-permute-start.3 = (f32[1,34,2048]{2,1,0:T(8,128)S(1)}, f32[1,34,2048]{2,1,0:T(8,128)S(1)}, u32[]{:S(2)}, u32[]{:S(2)}) collective-permute-start(f32[1,34,2048]{2,1,0:T(8,128)S(1)} %get-tuple-element.5), channel_id=1, source_target_pairs={{1,0},{2,1},{3,2},{4,3},{5,4},{6,5},{7,6},{9,8},{10,9},{11,10},{12... | collective-permute-start | bytes 835592 | tf_op jit(solution)/shard_map/ppermute | solution.py:19
  32.9 7.6 %collective-permute-start.4 = (f32[8,1,2048]{2,0,1:T(8,128)S(1)}, f32[8,1,2048]{2,0,1:T(8,128)S(1)}, u32[]{:S(2)}, u32[]{:S(2)}) collective-permute-start(f32[8,1,2048]{2,0,1:T(8,128)S(1)} %copy.90), channel_id=1, source_target_pairs={{0,8},{8,16},{16,24},{1,9},{9,17},{17,25},{2,10},{10,18},{18,26},{... | collective-permute-start | bytes 196616 | tf_op jit(solution)/shard_map/ppermute | solution.py:17
  39.1 3.1 %collective-permute-start.5 = (f32[8,1,2048]{2,0,1:T(8,128)S(1)}, f32[8,1,2048]{2,0,1:T(8,128)S(1)}, u32[]{:S(2)}, u32[]{:S(2)}) collective-permute-start(f32[8,1,2048]{2,0,1:T(8,128)S(1)} %copy.91), channel_id=1, source_target_pairs={{8,0},{16,8},{24,16},{9,1},{17,9},{25,17},{10,2},{18,10},{26,18},{... | collective-permute-start | bytes 196616 | tf_op jit(solution)/shard_map/ppermute | solution.py:19
  42.5 10.6 %collective-permute-start.6 = (f32[1,34,2048]{2,1,0:T(8,128)S(1)}, f32[1,34,2048]{2,1,0:T(8,128)S(1)}, u32[]{:S(2)}, u32[]{:S(2)}) collective-permute-start(f32[1,34,2048]{2,1,0:T(8,128)S(1)} %get-tuple-element.2), channel_id=1, source_target_pairs={{0,1},{1,2},{2,3},{3,4},{4,5},{5,6},{6,7},{8,9},{9,10},{10,11},{11... | collective-permute-start | bytes 835592 | tf_op jit(solution)/shard_map/ppermute | solution.py:17
  46.6 14.8 %copy-start.5 = (f32[8,32,2048]{2,1,0:T(8,128)S(1)}, f32[8,32,2048]{2,1,0:T(8,128)}, u32[]{:S(2)}) copy-start(f32[8,32,2048]{2,1,0:T(8,128)} %param.9) | copy-start | bytes 6291460
  46.6 11.7 %collective-permute-start.7 = (f32[1,34,2048]{2,1,0:T(8,128)S(1)}, f32[1,34,2048]{2,1,0:T(8,128)S(1)}, u32[]{:S(2)}, u32[]{:S(2)}) collective-permute-start(f32[1,34,2048]{2,1,0:T(8,128)S(1)} %get-tuple-element.3), channel_id=1, source_target_pairs={{1,0},{2,1},{3,2},{4,3},{5,4},{6,5},{7,6},{9,8},{10,9},{11,10},{12... | collective-permute-start | bytes 835592 | tf_op jit(solution)/shard_map/ppermute | solution.py:19
  162.6 4.5 %copy-start.6 = (s32[32,256]{1,0:T(8,128)S(1)}, s32[32,256]{1,0:T(8,128)}, u32[]{:S(2)}) copy-start(s32[32,256]{1,0:T(8,128)} %param.12) | copy-start | bytes 98308
  162.6 51.8 %all-to-all-start.1 = ((f32[64,32,256]{2,1,0:T(8,128)}), f32[64,32,256]{2,1,0:T(8,128)}, u32[]{:S(2)}, u32[]{:S(2)}) async-start(f32[64,32,256]{2,1,0:T(8,128)} %copy.98), calls=%async_computation.1 | async-start | bytes 4194304 | tf_op jit(solution)/shard_map/all_to_all | solution.py:66
where the time goes:
time: 218 us
  waiting for transfers between devices  71.9 us (33%)
  blocking collectives  59.5 us (27%)
  local copies, waits for them, and re-layouts  32.9 us (15%)
  starting transfers between devices  26.2 us (12%)
  other arithmetic  22.6 us (10%)
  matrix products  3.6 us (2%)
    all_to_all x1, blocking collectives, body(): lax.all_to_all(current_tracer_values, 'tile', split_axis=2, concat_axis=0...  59.5 us
    all_to_all x1, waiting for transfers between devices, body(): lax.all_to_all(smoothed_field, 'tile', split_axis=0, concat_axis=2, tiled...  46.7 us
    ppermute x4, starting transfers between devices, with_halo(): lax.ppermute(tail, axis, [(i, (i + 1) % count) for i in range(ends)])  16.1 us
    ppermute x4, waiting for transfers between devices, with_halo(): lax.ppermute(head, axis, [((i + 1) % count, i) for i in range(ends)])  15.8 us
    unnamed x18, local copies, waits for them, and re-layouts  13.5 us
    ppermute x4, waiting for transfers between devices, with_halo(): lax.ppermute(tail, axis, [(i, (i + 1) % count) for i in range(ends)])  9.4 us
    mul x2, other arithmetic, advance(): wet_cells * (center + misfit + change + 0.1 * lateral + 0.15 * vertical)  7.31 us
    all_to_all x1, other arithmetic, body(): lax.all_to_all(current_tracer_values, 'tile', split_axis=2, concat_axis=0...  7.22 us
  transfers between devices with their start and end apart: 9, of which 7 were waited for; matrix products, arithmetic and copies ran while one was open for 0% of the time, Pallas kernels for 0%

commit v1 on v0

--- a/solution.py
+++ b/solution.py
@@ -60,7 +60,15 @@
         bordered = with_halo(current_tracer_values, (("grp", 1), ("tile", 0)), 1)
         padded = jnp.pad(bordered, ((0, 0), (0, 0), (1, 1)))
         current_tracer_values = advance(padded, misfit, east_speed, north_speed, wet_cells)
-    pencil = lax.all_to_all(current_tracer_values, "tile", split_axis=2, concat_axis=0, tiled=True)
+    pencil = jnp.concatenate(
+        jax.lax.all_to_all(
+            jnp.stack(jnp.split(current_tracer_values, jax.lax.axis_size("tile"), axis=2)),
+            "tile",
+            0,
+            0,
+        ),
+        axis=0,
+    )
     smoothed_field = smooth_levels(vertical_filter_matrix, pencil)
     surface_layer = smoothed_field[0]
     filtered_thermal_sensitivity = lax.all_to_all(

time: 218 us -> 185 us (0.85)
  local copies, waits for them, and re-layouts: 32.9 us -> 7.49 us
  other arithmetic: 22.6 us -> 15.4 us
    unnamed x18 -> x21, local copies, waits for them, and re-layouts: 13.5 us -> 0.18 us
    all_to_all x1 -> x0, other arithmetic: 7.22 us -> none  [body(): lax.all_to_all(current_tracer_values, 'tile', split_axis=2, concat_axis=0...]
    all_to_all x2 -> x0, local copies, waits for them, and re-layouts: 7.09 us -> none  [body(): lax.all_to_all(current_tracer_values, 'tile', split_axis=2, concat_axis=0...]
    mul x1 -> x0, local copies, waits for them, and re-layouts: 4.74 us -> none  [advance(): wet_cells * (center + misfit + change + 0.1 * lateral + 0.15 * vertical)]
where the time goes in v1:
time: 185 us
  waiting for transfers between devices  72 us (39%)
  blocking collectives  59.4 us (32%)
  starting transfers between devices  26.1 us (14%)
  other arithmetic  15.4 us (8%)
  local copies, waits for them, and re-layouts  7.49 us (4%)
  matrix products  3.26 us (2%)
    all_to_all x1, blocking collectives, body(): jax.lax.all_to_all(jnp.stack(jnp.split(current_tracer_values, jax.lax.axi...  59.4 us
    all_to_all x1, waiting for transfers between devices, body(): lax.all_to_all(smoothed_field, 'tile', split_axis=0, concat_axis=2, tiled...  46.7 us
    ppermute x4, starting transfers between devices, with_halo(): lax.ppermute(tail, axis, [(i, (i + 1) % count) for i in range(ends)])  16.1 us
    ppermute x4, waiting for transfers between devices, with_halo(): lax.ppermute(head, axis, [((i + 1) % count, i) for i in range(ends)])  16 us
    ppermute x4, waiting for transfers between devices, with_halo(): lax.ppermute(tail, axis, [(i, (i + 1) % count) for i in range(ends)])  9.4 us
    mul x2, other arithmetic, advance(): wet_cells * (center + misfit + change + 0.1 * lateral + 0.15 * vertical)  7.31 us
    concatenate x2, other arithmetic, with_halo(): jnp.concatenate([lax.ppermute(tail, axis, [(i, (i + 1) % count) for i in...  6.23 us
    ppermute x4, starting transfers between devices, with_halo(): lax.ppermute(head, axis, [((i + 1) % count, i) for i in range(ends)])  5.56 us
  transfers between devices with their start and end apart: 9, of which 7 were waited for; matrix products, arithmetic and copies ran while one was open for 0% of the time, Pallas kernels for 0%

profile of v1, /device:TPU:0, one launch (start us, length us, event | category | flops | bytes accessed | tf_op | source)
XLA Modules:
  0.0 184.7 jit_solution(6528239351738529636)
XLA Ops:
  0.7 1.4 fusion.27
  2.1 2.4 %collective-permute-start = (f32[8,1,2048]{2,1,0:T(1,128)S(1)}, f32[8,1,2048]{2,1,0:T(1,128)S(1)}, u32[]{:S(2)}, u32[]{:S(2)}) collective-permute-start(f32[8,1,2048]{2,1,0:T(1,128)S(1)} %get-tuple-element.8), channel_id=1, source_target_pairs={{0,8},{8,16},{16,24},{1,9},{9,17},{17,25},{2,10},{10,18},{18,26},{... | collective-permute-start | bytes 196616 | tf_op jit(solution)/shard_map/ppermute | solution.py:17
  4.5 1.3 collective-permute-start.1
  5.8 4.0 %collective-permute-done.1 = f32[8,1,2048]{2,1,0:T(1,128)S(1)} collective-permute-done((f32[8,1,2048]{2,1,0:T(1,128)S(1)}, f32[8,1,2048]{2,1,0:T(1,128)S(1)}, u32[]{:S(2)}, u32[]{:S(2)}) %collective-permute-start.1) | collective-permute-done | bytes 65568 | tf_op jit(solution)/shard_map/ppermute | solution.py:19
  10.9 3.4 %collective-permute-start.2 = (f32[1,34,2048]{2,1,0:T(8,128)S(1)}, f32[1,34,2048]{2,1,0:T(8,128)S(1)}, u32[]{:S(2)}, u32[]{:S(2)}) collective-permute-start(f32[1,34,2048]{2,1,0:T(8,128)S(1)} %get-tuple-element.4), channel_id=1, source_target_pairs={{0,1},{1,2},{2,3},{3,4},{4,5},{5,6},{6,7},{8,9},{9,10},{10,11},{11... | collective-permute-start | bytes 835592 | tf_op jit(solution)/shard_map/ppermute | solution.py:17
  14.3 1.6 collective-permute-start.3
  15.9 4.3 %collective-permute-done.2 = f32[1,34,2048]{2,1,0:T(8,128)S(1)} collective-permute-done((f32[1,34,2048]{2,1,0:T(8,128)S(1)}, f32[1,34,2048]{2,1,0:T(8,128)S(1)}, u32[]{:S(2)}, u32[]{:S(2)}) %collective-permute-start.2) | collective-permute-done | bytes 278560 | tf_op jit(solution)/shard_map/ppermute | solution.py:17
  20.2 5.0 %collective-permute-done.3 = f32[1,34,2048]{2,1,0:T(8,128)S(1)} collective-permute-done((f32[1,34,2048]{2,1,0:T(8,128)S(1)}, f32[1,34,2048]{2,1,0:T(8,128)S(1)}, u32[]{:S(2)}, u32[]{:S(2)}) %collective-permute-start.3) | collective-permute-done | bytes 278560 | tf_op jit(solution)/shard_map/ppermute | solution.py:19
  25.2 3.1 %select_maximum_fusion.4 = f32[10,34,2050]{2,1,0:T(8,128)S(1)} fusion(f32[1,34,2048]{2,1,0:T(8,128)S(1)} %collective-permute-done.3, f32[1,34,2048]{2,1,0:T(8,128)S(1)} %collective-permute-done.2, f32[8,1,2048]{2,1,0:T(1,128)S(1)} %collective-permute-done.1, f32[8,32,2048]{2,1,0:T(8,128)S(1)} %copy-done.1, f32[8,1,2048]{2,1,0:T(1,128)S(1)} %collective-permute-done), kind=kLoop, calls=%fused_computation.6 | loop fusion | flops 8364000 | bytes 5573280 | tf_op jit(solution)/shard_map/concatenate | solution.py:15
  28.3 4.3 %fusion.10 = f32[8,32,2048]{2,1,0:T(8,128)S(1)} fusion(f32[1,34,2048]{2,1,0:T(8,128)S(1)} %collective-permute-done.3, f32[8,1,2048]{2,1,0:T(1,128)S(1)} %collective-permute-done.1, f32[8,32,2048]{2,1,0:T(8,128)S(1)} %copy-done.1, f32[8,1,2048]{2,1,0:T(1,128)S(1)} %collective-permute-done, f32[1,34,2048]{2,1,0:T(8,128)S(1)} %collective-permute-done.2, ...), kind=kLoop, calls=%fused_computation.29 | loop fusion | flops 16252928 | bytes 17465344 | tf_op jit(solution)/shard_map/mul | solution.py:39
  32.7 6.2 %collective-permute-start.4 = (f32[8,1,2048]{2,1,0:T(1,128)S(1)}, f32[8,1,2048]{2,1,0:T(1,128)S(1)}, u32[]{:S(2)}, u32[]{:S(2)}) collective-permute-start(f32[8,1,2048]{2,1,0:T(1,128)S(1)} %get-tuple-element.6), channel_id=1, source_target_pairs={{0,8},{8,16},{16,24},{1,9},{9,17},{17,25},{2,10},{10,18},{18,26},{... | collective-permute-start | bytes 196616 | tf_op jit(solution)/shard_map/ppermute | solution.py:17
  40.3 1.8 collective-permute-done.5
  42.2 4.1 %collective-permute-start.6 = (f32[1,34,2048]{2,1,0:T(8,128)S(1)}, f32[1,34,2048]{2,1,0:T(8,128)S(1)}, u32[]{:S(2)}, u32[]{:S(2)}) collective-permute-start(f32[1,34,2048]{2,1,0:T(8,128)S(1)} %get-tuple-element.2), channel_id=1, source_target_pairs={{0,1},{1,2},{2,3},{3,4},{4,5},{5,6},{6,7},{8,9},{9,10},{10,11},{11... | collective-permute-start | bytes 835592 | tf_op jit(solution)/shard_map/ppermute | solution.py:17
  46.3 1.4 collective-permute-start.7
  47.7 5.1 %collective-permute-done.6 = f32[1,34,2048]{2,1,0:T(8,128)S(1)} collective-permute-done((f32[1,34,2048]{2,1,0:T(8,128)S(1)}, f32[1,34,2048]{2,1,0:T(8,128)S(1)}, u32[]{:S(2)}, u32[]{:S(2)}) %collective-permute-start.6) | collective-permute-done | bytes 278560 | tf_op jit(solution)/shard_map/ppermute | solution.py:17
  52.8 5.2 %collective-permute-done.7 = f32[1,34,2048]{2,1,0:T(8,128)S(1)} collective-permute-done((f32[1,34,2048]{2,1,0:T(8,128)S(1)}, f32[1,34,2048]{2,1,0:T(8,128)S(1)}, u32[]{:S(2)}, u32[]{:S(2)}) %collective-permute-start.7) | collective-permute-done | bytes 278560 | tf_op jit(solution)/shard_map/ppermute | solution.py:19
  58.0 3.1 %select_maximum_fusion = f32[10,34,2050]{2,1,0:T(8,128)S(1)} fusion(f32[1,34,2048]{2,1,0:T(8,128)S(1)} %collective-permute-done.7, f32[1,34,2048]{2,1,0:T(8,128)S(1)} %collective-permute-done.6, f32[8,1,2048]{2,1,0:T(1,128)S(1)} %collective-permute-done.5, f32[8,32,2048]{2,1,0:T(8,128)S(1)} %fusion.10, f32[8,1,2048]{2,1,0:T(1,128)S(1)} %collective-permute-done.4), kind=kLoop, calls=%fused_computation.2 | loop fusion | flops 8364000 | bytes 5573280 | tf_op jit(solution)/shard_map/concatenate | solution.py:15
  61.1 3.0 %fusion.5 = f32[8,32,2048]{2,1,0:T(8,128)S(1)} fusion(f32[1,34,2048]{2,1,0:T(8,128)S(1)} %collective-permute-done.7, f32[8,1,2048]{2,1,0:T(1,128)S(1)} %collective-permute-done.5, f32[8,32,2048]{2,1,0:T(8,128)S(1)} %fusion.10, f32[8,1,2048]{2,1,0:T(1,128)S(1)} %collective-permute-done.4, f32[1,34,2048]{2,1,0:T(8,128)S(1)} %collective-permute-done.6, ...), kind=kLoop, calls=%fused_computation.16 | loop fusion | flops 16252928 | bytes 17465344 | tf_op jit(solution)/shard_map/mul | solution.py:39
  64.4 59.4 %all_to_all.23 = f32[8,8,32,256]{3,2,1,0:T(8,128)S(1)} all-to-all(f32[8,8,32,256]{3,2,1,0:T(8,128)S(1)} %fusion.17), channel_id=1, replica_groups=mesh['grp'=4,'tile'=8] {'tile'}, dimensions={0} | all-to-all | bytes 4194304 | tf_op jit(solution)/shard_map/all_to_all | solution.py:64
  123.8 3.3 %fusion.14 = f32[64,32,256]{2,0,1:T(8,128)S(1)} fusion(f32[8,8,32,256]{3,2,1,0:T(8,128)S(1)} %all_to_all.23, f32[64,64]{1,0:T(8,128)S(1)} %copy-done), kind=kOutput, calls=%fused_computation.40 | convolution fusion | flops 402653184 | bytes 4210688 | tf_op jit(solution)/shard_map/cz,zne->cne/dot_general | solution.py:43
  127.1 2.5 %copy.12 = f32[64,32,256]{2,1,0:T(8,128)} copy(f32[64,32,256]{2,0,1:T(8,128)S(1)} %fusion.14) | data formatting | bytes 4194304 | tf_op jit(solution)/shard_map/cz,zne->cne/dot_general | solution.py:43
  129.6 4.5 %all-to-all-start.1 = ((f32[64,32,256]{2,1,0:T(8,128)}), f32[64,32,256]{2,1,0:T(8,128)}, u32[]{:S(2)}, u32[]{:S(2)}) async-start(f32[64,32,256]{2,1,0:T(8,128)} %copy.12), calls=%async_computation.1 | async-start | bytes 4194304 | tf_op jit(solution)/shard_map/all_to_all | solution.py:74
  134.8 46.7 %all-to-all-done.1 = f32[64,32,256]{2,1,0:T(8,128)} async-done(((f32[64,32,256]{2,1,0:T(8,128)}), f32[64,32,256]{2,1,0:T(8,128)}, u32[]{:S(2)}, u32[]{:S(2)}) %all-to-all-start.1) | async-done | bytes 2097184 | tf_op jit(solution)/shard_map/all_to_all | solution.py:74
  181.5 3.2 %copy.15 = f32[8,8,4,8,256]{4,3,0,2,1:T(8,128)} copy(f32[8,8,4,8,256]{4,3,2,1,0:T(8,128)} %bitcast.15) | data formatting | bytes 4194304 | tf_op jit(solution)/shard_map/all_to_all | solution.py:74
  (30 shorter events, 3.4 us)
Async XLA Ops:
  0.6 123.2 %copy-start = (f32[64,64]{1,0:T(8,128)S(1)}, f32[64,64]{1,0:T(8,128)}, u32[]{:S(2)}) copy-start(f32[64,64]{1,0:T(8,128)} %param.13) | copy-start | bytes 49156
  0.6 24.6 %copy-start.1 = (f32[8,32,2048]{2,1,0:T(8,128)S(1)}, f32[8,32,2048]{2,1,0:T(8,128)}, u32[]{:S(2)}) copy-start(f32[8,32,2048]{2,1,0:T(8,128)} %param.7) | copy-start | bytes 6291460
  2.1 3.7 %collective-permute-start = (f32[8,1,2048]{2,1,0:T(1,128)S(1)}, f32[8,1,2048]{2,1,0:T(1,128)S(1)}, u32[]{:S(2)}, u32[]{:S(2)}) collective-permute-start(f32[8,1,2048]{2,1,0:T(1,128)S(1)} %get-tuple-element.8), channel_id=1, source_target_pairs={{0,8},{8,16},{16,24},{1,9},{9,17},{17,25},{2,10},{10,18},{18,26},{... | collective-permute-start | bytes 196616 | tf_op jit(solution)/shard_map/ppermute | solution.py:17
  4.5 5.3 %collective-permute-start.1 = (f32[8,1,2048]{2,1,0:T(1,128)S(1)}, f32[8,1,2048]{2,1,0:T(1,128)S(1)}, u32[]{:S(2)}, u32[]{:S(2)}) collective-permute-start(f32[8,1,2048]{2,1,0:T(1,128)S(1)} %get-tuple-element.9), channel_id=1, source_target_pairs={{8,0},{16,8},{24,16},{9,1},{17,9},{25,17},{10,2},{18,10},{26,18},{... | collective-permute-start | bytes 196616 | tf_op jit(solution)/shard_map/ppermute | solution.py:19
  10.9 9.3 %collective-permute-start.2 = (f32[1,34,2048]{2,1,0:T(8,128)S(1)}, f32[1,34,2048]{2,1,0:T(8,128)S(1)}, u32[]{:S(2)}, u32[]{:S(2)}) collective-permute-start(f32[1,34,2048]{2,1,0:T(8,128)S(1)} %get-tuple-element.4), channel_id=1, source_target_pairs={{0,1},{1,2},{2,3},{3,4},{4,5},{5,6},{6,7},{8,9},{9,10},{10,11},{11... | collective-permute-start | bytes 835592 | tf_op jit(solution)/shard_map/ppermute | solution.py:17
  14.3 14.0 %copy-start.2 = (f32[8,32,2048]{2,1,0:T(8,128)S(1)}, f32[8,32,2048]{2,1,0:T(8,128)}, u32[]{:S(2)}) copy-start(f32[8,32,2048]{2,1,0:T(8,128)} %param.8) | copy-start | bytes 6291460
  14.3 14.0 %copy-start.3 = (s32[8,32,2048]{2,1,0:T(8,128)S(1)}, s32[8,32,2048]{2,1,0:T(8,128)}, u32[]{:S(2)}) copy-start(s32[8,32,2048]{2,1,0:T(8,128)} %param.11) | copy-start | bytes 6291460
  14.3 14.0 %copy-start.4 = (f32[8,32,2048]{2,1,0:T(8,128)S(1)}, f32[8,32,2048]{2,1,0:T(8,128)}, u32[]{:S(2)}) copy-start(f32[8,32,2048]{2,1,0:T(8,128)} %param.10) | copy-start | bytes 6291460
  14.3 10.9 %collective-permute-start.3 = (f32[1,34,2048]{2,1,0:T(8,128)S(1)}, f32[1,34,2048]{2,1,0:T(8,128)S(1)}, u32[]{:S(2)}, u32[]{:S(2)}) collective-permute-start(f32[1,34,2048]{2,1,0:T(8,128)S(1)} %get-tuple-element.5), channel_id=1, source_target_pairs={{1,0},{2,1},{3,2},{4,3},{5,4},{6,5},{7,6},{9,8},{10,9},{11,10},{12... | collective-permute-start | bytes 835592 | tf_op jit(solution)/shard_map/ppermute | solution.py:19
  32.7 7.5 %collective-permute-start.4 = (f32[8,1,2048]{2,1,0:T(1,128)S(1)}, f32[8,1,2048]{2,1,0:T(1,128)S(1)}, u32[]{:S(2)}, u32[]{:S(2)}) collective-permute-start(f32[8,1,2048]{2,1,0:T(1,128)S(1)} %get-tuple-element.6), channel_id=1, source_target_pairs={{0,8},{8,16},{16,24},{1,9},{9,17},{17,25},{2,10},{10,18},{18,26},{... | collective-permute-start | bytes 196616 | tf_op jit(solution)/shard_map/ppermute | solution.py:17
  38.9 3.1 %collective-permute-start.5 = (f32[8,1,2048]{2,1,0:T(1,128)S(1)}, f32[8,1,2048]{2,1,0:T(1,128)S(1)}, u32[]{:S(2)}, u32[]{:S(2)}) collective-permute-start(f32[8,1,2048]{2,1,0:T(1,128)S(1)} %get-tuple-element.7), channel_id=1, source_target_pairs={{8,0},{16,8},{24,16},{9,1},{17,9},{25,17},{10,2},{18,10},{26,18},{... | collective-permute-start | bytes 196616 | tf_op jit(solution)/shard_map/ppermute | solution.py:19
  42.2 10.6 %collective-permute-start.6 = (f32[1,34,2048]{2,1,0:T(8,128)S(1)}, f32[1,34,2048]{2,1,0:T(8,128)S(1)}, u32[]{:S(2)}, u32[]{:S(2)}) collective-permute-start(f32[1,34,2048]{2,1,0:T(8,128)S(1)} %get-tuple-element.2), channel_id=1, source_target_pairs={{0,1},{1,2},{2,3},{3,4},{4,5},{5,6},{6,7},{8,9},{9,10},{10,11},{11... | collective-permute-start | bytes 835592 | tf_op jit(solution)/shard_map/ppermute | solution.py:17
  46.3 14.8 %copy-start.5 = (f32[8,32,2048]{2,1,0:T(8,128)S(1)}, f32[8,32,2048]{2,1,0:T(8,128)}, u32[]{:S(2)}) copy-start(f32[8,32,2048]{2,1,0:T(8,128)} %param.9) | copy-start | bytes 6291460
  46.3 11.7 %collective-permute-start.7 = (f32[1,34,2048]{2,1,0:T(8,128)S(1)}, f32[1,34,2048]{2,1,0:T(8,128)S(1)}, u32[]{:S(2)}, u32[]{:S(2)}) collective-permute-start(f32[1,34,2048]{2,1,0:T(8,128)S(1)} %get-tuple-element.3), channel_id=1, source_target_pairs={{1,0},{2,1},{3,2},{4,3},{5,4},{6,5},{7,6},{9,8},{10,9},{11,10},{12... | collective-permute-start | bytes 835592 | tf_op jit(solution)/shard_map/ppermute | solution.py:19
  129.6 4.5 %copy-start.6 = (s32[32,256]{1,0:T(8,128)S(1)}, s32[32,256]{1,0:T(8,128)}, u32[]{:S(2)}) copy-start(s32[32,256]{1,0:T(8,128)} %param.12) | copy-start | bytes 98308
  129.6 51.8 %all-to-all-start.1 = ((f32[64,32,256]{2,1,0:T(8,128)}), f32[64,32,256]{2,1,0:T(8,128)}, u32[]{:S(2)}, u32[]{:S(2)}) async-start(f32[64,32,256]{2,1,0:T(8,128)} %copy.12), calls=%async_computation.1 | async-start | bytes 4194304 | tf_op jit(solution)/shard_map/all_to_all | solution.py:74
